TPU v7x, 32 devices: a whole 2x2x4 slice. The times are simulated.
32 devices in a mesh: dev: 32 (over z, y, x, core).
Axes of the slice: x: 2, y: 2, z: 4, core: 2. Of those that a mesh axis runs over, the one named last changes fastest.
Arguments:
- moles: float32 [18, 2048, 1024], P(None, 'dev'), may hold values from 0.1 to 1
- old_content: float32 [18, 2048, 1024], P(None, 'dev'), may hold values from 0 to 1
- pressure: float32 [2048, 1024], P('dev'), may hold values from 0.5 to 1
- perm: float32 [2048, 1024], P('dev'), may hold values from 0.1 to 10
- labels: int32 [2048, 1024], P('dev'), may hold values from 0 to 1
- roots: int32 [2048, 1024], P('dev'), may hold values from 0 to 1
- counts: int32 [32], P('dev'), may hold values from 1 to 128, 2048 in all
- block_ids: int32 [4096], P('dev'), may hold values from 0 to 511, as said below
- wilson: float32 [18], replicated, may hold values from -1.5 to 1.5
- attraction: float32 [18, 18], replicated, may hold values from 0.3 to 0.9
- covolume: float32 [18], replicated, may hold values from 0.03 to 0.08
Outputs:
- residual: float32 [18, 2048, 1024], P(None, 'dev')
- pressure_step: float32 [2048, 1024], P('dev')
- vapour_fraction: float32 [2048, 1024], P('dev')
Inputs may be any that keep to these rules, and one draw needn't show every extreme that they name: counts sum to 2048; each device holds at least one two-phase block and at most 128, exactly 128 on some device. `block_ids`: each device's 128 entries are distinct block numbers of that device.
All inputs are finite; a program needn't handle non-finite values.
Results may differ from a plain program's by a relative error of at most 0.0003.
Values sent between devices are 32-bit elements; how exact they have to be, the bound alone decides.
No kernel may reach another device: no remote copies, remote signals or barrier semaphores. Data moves between devices by JAX's collectives and lax.ppermute only.
A program may use at most 128 MiB of HBM per device.

v0:
```python
import math

import jax
import jax.numpy as jnp
from jax import lax
from jax.experimental import pallas as pl
from jax.experimental.pallas import tpu as pltpu
from jax.sharding import PartitionSpec as P

BLK = 128
SUB = 8
SS_ITERS = 3
RR_ITERS = 3
Z_ITERS = 5
WIDE = 8
LOG2E = math.log2(math.e)
CELLS_VMEM = 32 * 1024 * 1024
FLUX_VMEM = 32 * 1024 * 1024

SQRT_TWO = math.sqrt(2.0)
TIME_STEP = 0.5
RELAX = 0.7
STEP_SCALE = 10.0
OFF_SCALE = RELAX * TIME_STEP

EDGE_PRES, EDGE_PERM, EDGE_LAM, EDGE_CSUM, EDGE_OSUM = range(5)
EDGE_PRES2, EDGE_PERM2, EDGE_LAM2 = range(5, 8)
EDGE_ROWS = 8
EDGE_SPAN = 32
AUX_IN, AUX_LEFT, AUX_RIGHT, AUX_FIRST, AUX_GAIN, AUX_STEP, AUX_ROW, AUX_DIAG = range(8)
AUX_ROWS = 8


def keep_in(space, *arrays):
    return [pltpu.with_memory_space_constraint(x, space) for x in arrays]


def recip(value):
    return pltpu.reciprocal(value, approx=True)


def odd_tiles(rows):
    return rows + SUB if (rows // SUB) % 2 == 0 else rows


def split_halves(value):
    high = value.astype(jnp.bfloat16)
    low = (value - high.astype(jnp.float32)).astype(jnp.bfloat16)
    return high, low


def widen(wide, attraction, covolume, comps):
    cols = comps * SUB
    group = lax.broadcasted_iota(jnp.int32, (comps, cols), 1) // SUB
    spread = jnp.where(group == lax.broadcasted_iota(jnp.int32, (comps, cols), 0), 1.0, 0.0)
    table = attraction[...]
    coefficients = 0.5 * (
        lax.dot_general(table, spread, (((1,), (0,)), ((), ())), precision=lax.Precision.HIGHEST)
        + lax.dot_general(table, spread, (((0,), (0,)), ((), ())), precision=lax.Precision.HIGHEST)
    )
    lane = lax.broadcasted_iota(jnp.int32, (SUB, cols), 1)
    row = lax.broadcasted_iota(jnp.int32, (SUB, cols), 0)
    diagonal = lane - (lane // SUB) * SUB == row
    zero = jnp.zeros((SUB, cols), jnp.float32)
    of_cov = zero
    for j in range(comps):
        of_cov = jnp.where(lane // SUB == j, covolume[j], of_cov)
    blocks = [coefficients[i : i + 1, :] for i in range(comps)] + [of_cov, zero + 1.0]
    for pair in range(len(blocks) // 2):
        rows = [jnp.where(diagonal, blocks[i], zero) for i in (2 * pair, 2 * pair + 1)]
        high, low = split_halves(jnp.concatenate(rows, 0))
        wide[2 * SUB * pair : 2 * SUB * (pair + 1), :] = jnp.concatenate([high, low, high], 1)


def rows_of(g):
    return slice(g * SUB, (g + 1) * SUB)


def cubic(big_a, big_b, vapour_flag):
    two_b = 2.0 * big_b
    two_b_square = two_b * big_b
    least = two_b + 0.01
    most = big_b + 2.0
    if vapour_flag is True:
        start, shift, factor = 1.0 + big_b, big_b + 0.5, -0.5 * big_a
    elif vapour_flag is False:
        start, shift, factor = 3.0 * big_b, big_b, 0.5 * recip(big_a)
    else:
        start = jnp.where(vapour_flag, 1.0 + big_b, 3.0 * big_b)
        shift = jnp.where(vapour_flag, big_b + 0.5, big_b)
        factor = jnp.where(vapour_flag, -0.5 * big_a, -0.5 * recip(big_a))
        base = jnp.where(vapour_flag, two_b, 1.0 + two_b)

    def step(w):
        spread = w * w - two_b_square
        if vapour_flag is True:
            part = factor * (w - two_b) * recip(spread)
        elif vapour_flag is False:
            part = spread * ((1.0 + two_b) - w) * factor
        else:
            part = factor * (w - base) * jnp.where(vapour_flag, recip(spread), spread)
        return jnp.minimum(jnp.maximum((0.5 * w + shift) + part, least), most)

    return start, step


def roots_of(*equations):
    steps = [cubic(*equation) for equation in equations]
    found = [start for start, _ in steps]
    for _ in range(Z_ITERS):
        found = [step(w) for w, (_, step) in zip(found, steps)]
    return [w - big_b for w, (_, big_b, _) in zip(found, equations)]


def cells_kernel(
    counts,
    block_ids_hbm,
    wilson_hbm,
    covolume_hbm,
    attraction_hbm,
    moles_hbm,
    old_hbm,
    pres_hbm,
    perm_hbm,
    labels_hbm,
    roots_hbm,
    edge_a,
    edge_b,
    held,
    old,
    mobile,
    pres,
    perm,
    lam,
    scale,
    csum,
    vap,
    pres_flat,
    perm_flat,
    labels,
    roots,
    w_wide,
    sums,
    pack,
    pack_pres,
    inv_excess,
    liquid,
    vapour,
    out_cell,
    found,
    block_ids,
    wilson,
    covolume,
    attraction,
    in_sem,
    old_sem,
    cell_sem,
    table_sem,
):
    comps, layers, face = moles_hbm.shape
    strips = face // BLK
    groups = layers // SUB
    padded = layers + 2 * SUB
    inside = slice(SUB, SUB + layers)

    def lanes_of(k):
        return pl.ds(pl.multiple_of(k * BLK, BLK), BLK)

    def strip_of(k):
        return pl.ds(pl.multiple_of(k * layers, SUB), layers)

    def strip_in(source, target, sem, k):
        return pltpu.make_async_copy(
            source.at[:, :, lanes_of(k)], target.at[:, strip_of(k), :], sem.at[k]
        )

    cell_copies = [
        pltpu.make_async_copy(pres_hbm, pres_flat, cell_sem.at[0]),
        pltpu.make_async_copy(roots_hbm, roots, cell_sem.at[1]),
        pltpu.make_async_copy(labels_hbm, labels, cell_sem.at[2]),
        pltpu.make_async_copy(perm_hbm, perm_flat, cell_sem.at[3]),
    ]
    table_copies = [
        pltpu.make_async_copy(source, target, table_sem.at[n])
        for n, (source, target) in enumerate(
            (
                (attraction_hbm, attraction),
                (covolume_hbm, covolume),
                (wilson_hbm, wilson),
                (block_ids_hbm, block_ids),
            )
        )
    ]
    for copy in table_copies + cell_copies:
        copy.start()
    for k in range(strips):
        strip_in(moles_hbm, held, in_sem, k).start()

    zero_tile = jnp.zeros((SUB, BLK), jnp.float32)
    zero_strip = jnp.zeros((padded, BLK), jnp.float32)

    for ref in (pres, perm, lam):
        for k in (0, strips + 1):
            ref[k] = zero_strip
        for k in range(1, strips + 1):
            ref[k, 0:SUB] = zero_tile
            ref[k, SUB + layers : padded] = zero_tile

    def clear(i, carry):
        for k in (0, strips + 1):
            mobile[i, k * padded : (k + 1) * padded, :] = zero_strip
        for k in range(1, strips + 1):
            mobile[i, k * padded : k * padded + SUB, :] = zero_tile
            mobile[i, (k + 1) * padded - SUB : (k + 1) * padded, :] = zero_tile
        return carry

    lax.fori_loop(0, comps, clear, 0)
    for copy in table_copies:
        copy.wait()
    widen(w_wide, attraction, covolume, comps)

    cols = comps * SUB

    def mixture(tile, count, keep=None):
        parts = ([], [], [])
        for g in range(0, count, 2):
            highs, lows = [], []
            for j in range(comps // 2):
                both = [
                    jnp.concatenate([tile(2 * j, at), tile(2 * j + 1, at)], 0) for at in (g, g + 1)
                ]
                high, low = split_halves(jnp.concatenate(both, 1))
                highs.append(high)
                lows.append(low)
            result = jnp.dot(
                w_wide[...],
                jnp.concatenate(highs + highs + lows, 0),
                preferred_element_type=jnp.float32,
            )
            if keep is not None:
                sums[:, (keep + g) * BLK : (keep + g + 2) * BLK] = result[0:cols]
            for n, at in enumerate((g, g + 1)):
                lanes = slice(n * BLK, (n + 1) * BLK)
                quad = tile(0, at) * result[0:SUB, lanes]
                for i in range(1, comps):
                    quad = quad + tile(i, at) * result[i * SUB : (i + 1) * SUB, lanes]
                parts[0].append(result[cols + SUB : cols + 2 * SUB, lanes])
                parts[1].append(result[cols : cols + SUB, lanes])
                parts[2].append(quad)
        return [jnp.concatenate(part, 0) for part in parts]

    def total(at, start, count):
        rows = slice(at * SUB, (at + 1) * SUB)
        return jnp.concatenate(
            [sums[rows, g * BLK : (g + 1) * BLK] for g in range(start, start + count)], 0
        )

    for copy in cell_copies:
        copy.wait()
    for k in range(strips):
        pres[k + 1, inside, :] = pres_flat[:, k * BLK : (k + 1) * BLK]
        perm[k + 1, inside, :] = perm_flat[:, k * BLK : (k + 1) * BLK]

    def padded_of(k):
        return pl.ds(pl.multiple_of((k + 1) * padded + SUB, SUB), layers)

    def single(k, carry):
        strip_in(moles_hbm, held, in_sem, k).wait()
        strip_in(old_hbm, old, old_sem, k).start()
        amount, b_sum, quad = mixture(
            lambda i, g: held[i, pl.ds(pl.multiple_of(k * layers + g * SUB, SUB), SUB), :], groups
        )
        pressure = pres[k + 1, inside, :]
        inv_amount = recip(amount)
        big_a = pressure * quad * inv_amount * inv_amount
        big_b = pressure * b_sum * inv_amount
        is_vapour = roots[:, lanes_of(k)] == 1
        (z_factor,) = roots_of((big_a, big_b, is_vapour))
        rho = pressure * recip(z_factor)
        part = labels[:, lanes_of(k)].astype(jnp.float32)
        move = ((1.0 - part) * (1.0 - part) + 4.0 * part * part) * rho
        vap[k] = part
        scale[k] = rho
        csum[k] = amount * rho
        lam[k + 1, inside, :] = amount * move
        for i in range(comps):
            mobile[i, padded_of(k), :] = held[i, strip_of(k), :] * move
        return carry

    lax.fori_loop(0, strips, single, 0)

    batch = WIDE * SUB
    own_count = counts[0]
    held_stride, mobile_stride, pack_stride = (ref.shape[1] for ref in (held, mobile, pack))
    held_rows = held.reshape(comps * held_stride, BLK)
    mobile_rows = mobile.reshape(comps * mobile_stride, BLK)
    pack_rows = pack.reshape(comps * pack_stride, BLK)
    liquid_rows = liquid.reshape(comps * pack_stride, BLK)
    vapour_rows = vapour.reshape(comps * pack_stride, BLK)
    bits = strips.bit_length() - 1

    def place(slot):
        block = block_ids[jnp.minimum(slot, own_count - 1)]
        layer = lax.shift_right_logical(block, bits)
        return block - lax.shift_left(layer, bits), layer

    def field_at(k, layer):
        return pl.ds(k * layers + layer, comps, stride=held_stride)

    def mobile_at(k, layer):
        return pl.ds((k + 1) * padded + layer + SUB, comps, stride=mobile_stride)

    def flash(number, carry):
        base = number * batch

        def gather(group, inner):
            for n in range(SUB):
                r = group * SUB + n
                k, layer = place(base + r)
                pack_rows[pl.ds(r, comps, stride=pack_stride), :] = held_rows[field_at(k, layer), :]
                pack_pres[pl.ds(r, 1), :] = pres[k + 1, pl.ds(layer + SUB, 1), :]
            return inner

        lax.fori_loop(0, WIDE, gather, 0)
        slots = slice(0, batch)
        pressure = pack_pres[...]
        amount = pack[0, slots, :]
        for i in range(1, comps):
            amount = amount + pack[i, slots, :]
        inv_amount = recip(amount)
        for i in range(comps):
            pack[i, slots, :] = pack[i, slots, :] * inv_amount

        def keep_k(i, log2_k):
            inv_excess[i, slots, :] = recip(jnp.exp2(log2_k) - 1.0)

        log2_pres = jnp.log(pressure) * LOG2E
        for i in range(comps):
            keep_k(i, wilson[i] * LOG2E - log2_pres)

        def newton(_, part):
            value = jnp.zeros((batch, BLK), jnp.float32)
            slope = jnp.full((batch, BLK), 0.05, jnp.float32)
            for i in range(comps):
                ratio = recip(inv_excess[i, slots, :] + part)
                term = pack[i, slots, :] * ratio
                value = value + term
                slope = slope + term * ratio
            return jnp.minimum(jnp.maximum(part + value * recip(slope), 0.0), 1.0)

        def sweep(number_of_sweep, inner):
            half = jnp.full((batch, BLK), 0.5, jnp.float32)
            part = lax.fori_loop(0, RR_ITERS, newton, half)
            for i in range(comps):
                fraction = pack[i, slots, :]
                term = fraction * recip(inv_excess[i, slots, :] + part)
                liq = fraction - part * term
                liquid[i, slots, :] = liq
                vapour[i, slots, :] = liq + term
            phases = []
            equations = []
            for n, (ref, flag) in enumerate(((liquid, False), (vapour, True))):
                whole, b_sum, quad = mixture(lambda i, g: ref[i, rows_of(g), :], WIDE, n * WIDE)
                inv_whole = recip(whole)
                b_mix = b_sum * inv_whole
                a_mix = quad * inv_whole * inv_whole
                big_b = pressure * b_mix
                equations.append((pressure * a_mix, big_b, flag))
                phases.append((quad, whole, inv_whole, a_mix, b_mix, big_b))
            factors = roots_of(*equations)
            found[0] = part
            for n in range(2):
                found[1 + n] = factors[n]
                found[3 + n] = phases[n][2]

            @pl.when(number_of_sweep + 1 < SS_ITERS)
            def _():
                parts = []
                for (quad, whole, _, a_mix, b_mix, big_b), z_factor in zip(phases, factors):
                    log_arg = (z_factor + (1.0 + SQRT_TWO) * big_b) * recip(
                        z_factor + (1.0 - SQRT_TWO) * big_b
                    )
                    inv_b = recip(b_mix)
                    depart = a_mix * inv_b * (1.0 / (2.0 * SQRT_TWO)) * jnp.log(log_arg)
                    of_cov = (LOG2E * inv_b) * (z_factor - 1.0 + depart)
                    of_sum = (2.0 * LOG2E) * depart * whole * recip(quad)
                    parts.append((of_cov, LOG2E * jnp.log(z_factor - big_b), of_sum))
                cov_gap = parts[0][0] - parts[1][0]
                log_gap = parts[0][1] - parts[1][1]
                for i in range(comps):
                    log2_k = (covolume[i] * cov_gap - log_gap) - (
                        parts[0][2] * total(i, 0, WIDE) - parts[1][2] * total(i, WIDE, WIDE)
                    )
                    keep_k(i, jnp.minimum(jnp.maximum(log2_k, -3.0 * LOG2E), 3.0 * LOG2E))
            return inner

        lax.fori_loop(0, SS_ITERS, sweep, 0)
        part = found[0]
        rho_liq = amount * pressure * recip(found[1])
        rho_vap = amount * pressure * recip(found[2])
        rest = 1.0 - part
        move_liq = rest * rest * rho_liq
        move_vap = 4.0 * part * part * rho_vap
        hold_liq = rest * rho_liq
        hold_vap = part * rho_vap
        out_cell[0] = part
        out_cell[1] = move_liq + move_vap
        out_cell[2] = hold_liq + hold_vap
        inv_liq, inv_vap = found[3], found[4]
        move_liq = move_liq * inv_liq
        move_vap = move_vap * inv_vap
        hold_liq = hold_liq * inv_liq
        hold_vap = hold_vap * inv_vap
        for i in range(comps):
            liq, gas = liquid[i, slots, :], vapour[i, slots, :]
            liquid[i, slots, :] = move_liq * liq + move_vap * gas
            vapour[i, slots, :] = hold_liq * liq + hold_vap * gas
        one_row = jnp.ones((1, BLK), jnp.float32)

        def scatter(group, inner):
            for n in range(SUB):
                r = group * SUB + n
                k, layer = place(base + r)
                of = pl.ds(r, comps, stride=pack_stride)
                mobile_rows[mobile_at(k, layer), :] = liquid_rows[of, :]
                held_rows[field_at(k, layer), :] = vapour_rows[of, :]
                one = pl.ds(r, 1)
                row = pl.ds(layer, 1)
                vap[k, row, :] = out_cell[0, one, :]
                lam[k + 1, pl.ds(layer + SUB, 1), :] = out_cell[1, one, :]
                csum[k, row, :] = out_cell[2, one, :]
                scale[k, row, :] = one_row
            return inner

        lax.fori_loop(0, WIDE, scatter, 0)
        return carry

    lax.fori_loop(0, (own_count + batch - 1) // batch, flash, 0)
    for k in range(strips):
        strip_in(old_hbm, old, old_sem, k).wait()
    old_rows = old.reshape(comps * old.shape[1], BLK)

    def edge_values(k, at, inner):
        here = slice(at, at + 1)
        pad_here = slice(SUB + at, SUB + at + 1)
        pad_inner = slice(SUB + inner, SUB + inner + 1)
        values = [None] * EDGE_ROWS
        values[EDGE_PRES] = pres[k + 1, pad_here, :]
        values[EDGE_PERM] = perm[k + 1, pad_here, :]
        values[EDGE_LAM] = lam[k + 1, pad_here, :]
        values[EDGE_CSUM] = csum[k, here, :]
        values[EDGE_OSUM] = jnp.sum(old_rows[field_at(k, at), :], 0, keepdims=True)
        values[EDGE_PRES2] = pres[k + 1, pad_inner, :]
        values[EDGE_PERM2] = perm[k + 1, pad_inner, :]
        values[EDGE_LAM2] = lam[k + 1, pad_inner, :]
        return [mobile_rows[mobile_at(k, at), :]] + values

    odd = lax.rem(lax.axis_index("dev"), 2) == 1
    for k in range(strips):
        lanes = slice(k * BLK, (k + 1) * BLK)
        tops = edge_values(k, 0, 1)
        lows = edge_values(k, layers - 1, layers - 2)
        row = 0
        for top, low in zip(tops, lows):
            rows = slice(row, row + top.shape[0])
            edge_a[rows, lanes] = jnp.where(odd, top, low)
            edge_b[rows, lanes] = jnp.where(odd, low, top)
            row = rows.stop


def flux_kernel(
    held,
    old,
    mobile,
    pres,
    perm,
    lam,
    scale,
    csum,
    vap,
    resid_hbm,
    step_hbm,
    vap_hbm,
    top_aux,
    low_aux,
    resid,
    first,
    row_sum,
    diag,
    weights,
    step,
    vap_flat,
    step_sem,
    vap_sem,
    out_sem,
):
    comps = held.shape[0]
    strips, layers, _ = scale.shape
    groups = layers // SUB
    padded = layers + 2 * SUB

    def lanes_of(k):
        return pl.ds(pl.multiple_of(k * BLK, BLK), BLK)

    def strip_out(k):
        return pltpu.make_async_copy(resid.at[:, k], resid_hbm.at[:, :, lanes_of(k)], out_sem.at[k])

    for k in range(strips):
        vap_flat[:, k * BLK : (k + 1) * BLK] = vap[k]
    vap_copy = pltpu.make_async_copy(vap_flat, vap_hbm, vap_sem)
    vap_copy.start()
    zero_tile = jnp.zeros((SUB, BLK), jnp.float32)
    for k in range(strips + 2):
        for g in range(groups + 2):
            if k in (0, strips + 1) or g in (0, groups + 1):
                first[k, rows_of(g), :] = zero_tile

    lane_index = lax.broadcasted_iota(jnp.int32, (SUB, BLK), 1)
    is_last_lane = lane_index == BLK - 1
    is_first_lane = lane_index == 0

    def around(load, k, g):
        at = SUB * (g + 1)
        here = load(k + 1, slice(at, at + SUB))
        up = load(k + 1, slice(at - 1, at + SUB - 1))
        down = load(k + 1, slice(at + 1, at + SUB + 1))
        before = load(k, slice(at, at + SUB))
        after = load(k + 2, slice(at, at + SUB))
        left = pltpu.roll(jnp.where(is_last_lane, before, here), 1, 1)
        right = pltpu.roll(jnp.where(is_first_lane, after, here), BLK - 1, 1)
        return here, (up, down, left, right)

    def fluxes(k, carry):
        for g in range(groups):
            rows = rows_of(g)
            p_here, p_near = around(lambda s, r: pres[s, r, :], k, g)
            k_here, k_near = around(lambda s, r: perm[s, r, :], k, g)
            l_here, l_near = around(lambda s, r: lam[s, r, :], k, g)
            drives = []
            couplings = []
            for n in range(4):
                transmiss = k_here * k_near[n] * recip(k_here + k_near[n])
                drives.append((TIME_STEP * transmiss) * (p_here - p_near[n]))
                couplings.append(transmiss * (l_here + l_near[n]))
            drive_sum = (drives[0] + drives[1]) + (drives[2] + drives[3])
            content_scale = scale[k, rows, :]
            flat_rows = pl.ds(pl.multiple_of(k * layers + g * SUB, SUB), SUB)
            row_total = zero_tile
            for i in range(comps):
                m_here, m_near = around(
                    lambda s, r, i=i: mobile[i, pl.ds(s * padded + r.start, SUB), :], k, g
                )
                value = held[i, flat_rows, :] * content_scale - old[i, flat_rows, :]
                value = value + drive_sum * m_here
                value = value + (drives[0] * m_near[0] + drives[1] * m_near[1])
                value = value + (drives[2] * m_near[2] + drives[3] * m_near[3])
                resid[i, k, rows, :] = value
                row_total = row_total + value
            diagonal = TIME_STEP * (
                (couplings[0] + couplings[1]) + (couplings[2] + couplings[3])
            ) + csum[k, rows, :] * recip(p_here)
            inv_diag = recip(diagonal)
            row_sum[k, rows, :] = row_total
            diag[k, rows, :] = diagonal
            first[k + 1, SUB * (g + 1) : SUB * (g + 2), :] = -row_total * inv_diag
            gain = (STEP_SCALE * OFF_SCALE) * inv_diag
            for n in range(4):
                weights[n, k, rows, :] = couplings[n] * gain
        strip_out(k).start()
        return carry

    lax.fori_loop(0, strips, fluxes, 0)

    def steps(k, carry):
        for g in range(groups):
            rows = rows_of(g)
            here, near = around(lambda s, r: first[s, r, :], k, g)
            step[rows, lanes_of(k)] = (
                STEP_SCALE * here
                + (weights[0, k, rows, :] * near[0] + weights[1, k, rows, :] * near[1])
                + (weights[2, k, rows, :] * near[2] + weights[3, k, rows, :] * near[3])
            )
        return carry

    lax.fori_loop(0, strips, steps, 0)
    step_copy = pltpu.make_async_copy(step, step_hbm, step_sem)
    step_copy.start()

    resid_rows = resid.reshape(comps * strips * layers, BLK)
    for aux, at, inner, toward, away in (
        (top_aux, 0, 1, 0, 1),
        (low_aux, layers - 1, layers - 2, 1, 0),
    ):
        for k in range(strips):
            lanes = slice(k * BLK, (k + 1) * BLK)
            here = slice(at, at + 1)
            behind = slice(inner, inner + 1)
            from_row = pl.ds(k * layers + at, comps, stride=strips * layers)
            aux[0:comps, lanes] = resid_rows[from_row, :]
            unscale = diag[k, here, :]
            values = [None] * AUX_ROWS
            values[AUX_IN] = weights[away, k, here, :] * unscale
            values[AUX_LEFT] = weights[2, k, here, :] * unscale
            values[AUX_RIGHT] = weights[3, k, here, :] * unscale
            values[AUX_FIRST] = first[k + 1, SUB + inner : SUB + inner + 1, :]
            values[AUX_GAIN] = weights[toward, k, behind, :]
            values[AUX_STEP] = step[behind, lanes]
            values[AUX_ROW] = row_sum[k, here, :]
            values[AUX_DIAG] = unscale
            for n, value in enumerate(values):
                aux[comps + n : comps + n + 1, lanes] = value
    vap_copy.wait()
    step_copy.wait()
    for k in range(strips):
        strip_out(k).wait()


def transmissibility(perm, perm_near):
    both = perm + perm_near
    return perm * perm_near / jnp.where(both == 0.0, 1.0, both)


def edge_kernel(
    edge_a,
    edge_b,
    top_aux,
    low_aux,
    in_even,
    in_odd,
    resid_in,
    step_in,
    resid_hbm,
    step_hbm,
    resid,
    step,
    sem,
):
    comps, layers, face = resid_hbm.shape
    odd = lax.rem(lax.axis_index("dev"), 2) == 1
    top_edge = jnp.where(odd, edge_a[...], edge_b[...])
    low_edge = jnp.where(odd, edge_b[...], edge_a[...])
    from_prev = jnp.where(odd, in_even[...], in_odd[...])
    from_next = jnp.where(odd, in_odd[...], in_even[...])
    copies = []
    for n, (edge, aux, other, at, inner) in enumerate(
        (
            (top_edge, top_aux, from_prev, 0, 1),
            (low_edge, low_aux, from_next, layers - 1, layers - 2),
        )
    ):

        def own(index):
            return edge[comps + index : comps + index + 1, :]

        def far(index):
            return other[comps + index : comps + index + 1, :]

        def near(index):
            return aux[comps + index : comps + index + 1, :]

        pres_far, perm_far, lam_far = far(EDGE_PRES), far(EDGE_PERM), far(EDGE_LAM)
        transmiss = transmissibility(own(EDGE_PERM), perm_far)
        drive = TIME_STEP * transmiss * (own(EDGE_PRES) - pres_far)
        lam_both = own(EDGE_LAM) + lam_far
        coupling = transmiss * lam_both
        row = near(AUX_ROW) + drive * lam_both
        diag = near(AUX_DIAG) + TIME_STEP * coupling
        first = -row / diag
        first_old = -near(AUX_ROW) / near(AUX_DIAG)
        row_far = far(EDGE_CSUM) - far(EDGE_OSUM) - drive * lam_both
        diag_far = coupling
        lane = lax.broadcasted_iota(jnp.int32, (1, face), 1)
        sides = [(far(EDGE_PRES2), far(EDGE_PERM2), far(EDGE_LAM2))]
        for shift, end in ((1, 0), (face - 1, face - 1)):
            pres_n, perm_n, lam_n = (pltpu.roll(x, shift, 1) for x in (pres_far, perm_far, lam_far))
            sides.append((pres_n, jnp.where(lane == end, 0.0, perm_n), lam_n))
        for pres_n, perm_n, lam_n in sides:
            joint = transmissibility(perm_far, perm_n) * (lam_far + lam_n)
            row_far = row_far + TIME_STEP * joint * (pres_far - pres_n)
            diag_far = diag_far + joint
        diag_far = TIME_STEP * diag_far + far(EDGE_CSUM) / jnp.where(pres_far == 0.0, 1.0, pres_far)
        first_far = -row_far / jnp.where(diag_far == 0.0, 1.0, diag_far)
        off = (
            (STEP_SCALE * OFF_SCALE) * coupling * first_far
            + near(AUX_IN) * near(AUX_FIRST)
            + near(AUX_LEFT) * pltpu.roll(first, 1, 1)
            + near(AUX_RIGHT) * pltpu.roll(first, face - 1, 1)
        )
        least = min(at, inner)
        step[n, at - least : at - least + 1, :] = STEP_SCALE * first + off / diag
        step[n, inner - least : inner - least + 1, :] = near(AUX_STEP) + near(AUX_GAIN) * (
            first - first_old
        )
        resid[n] = aux[0:comps, :] + drive * (edge[0:comps, :] + other[0:comps, :])
        for source, target in (
            (resid.at[n], resid_hbm.at[:, at, :]),
            (step.at[n, 0:2, :], step_hbm.at[least : least + 2, :]),
        ):
            copies.append(pltpu.make_async_copy(source, target, sem.at[len(copies)]))
            copies[-1].start()
    for copy in copies:
        copy.wait()


def on_device(
    moles,
    old_content,
    pressure,
    perm,
    labels,
    roots,
    counts,
    block_ids,
    wilson,
    attraction,
    covolume,
):
    comps, layers, face = moles.shape
    f32 = jnp.float32
    strips = face // BLK
    tables = (block_ids, wilson, covolume, attraction)
    rows_in = comps * SUB
    vmem = pl.BlockSpec(memory_space=pltpu.VMEM)
    hbm = pl.BlockSpec(memory_space=pltpu.HBM)
    padded = layers + 2 * SUB
    flat = pltpu.VMEM((layers, face), f32)
    flat_int = pltpu.VMEM((layers, face), jnp.int32)
    cell = pltpu.VMEM((strips, layers, BLK), f32)
    cell_pad = pltpu.VMEM((strips + 2, padded, BLK), f32)
    field = pltpu.VMEM((comps, odd_tiles(strips * layers), BLK), f32)
    field_pad = pltpu.VMEM((comps, odd_tiles((strips + 2) * padded), BLK), f32)
    packed = pltpu.VMEM((comps, odd_tiles(WIDE * SUB), BLK), f32)
    edge_shape = pltpu.VMEM((EDGE_SPAN, face), f32)
    aux_shape = pltpu.VMEM((comps + AUX_ROWS, face), f32)
    field_shape = jax.ShapeDtypeStruct((comps, layers, face), f32)
    cell_shape = jax.ShapeDtypeStruct((layers, face), f32)
    field_out = pltpu.VMEM((comps, strips, layers, BLK), f32)
    held_types = [field, field, field_pad] + [cell_pad] * 3 + [cell] * 3
    edge_a, edge_b, *state = pl.pallas_call(
        cells_kernel,
        out_shape=[edge_shape, edge_shape]
        + held_types,
        in_specs=[pl.BlockSpec(memory_space=pltpu.SMEM)] + [hbm] * 10,
        out_specs=[vmem] * (2 + len(held_types)),
        scratch_shapes=[flat, flat, flat_int, flat_int]
        + [pltpu.VMEM((rows_in + 2 * SUB, 3 * rows_in), jnp.bfloat16)]
        + [pltpu.VMEM((rows_in, 2 * WIDE * BLK), f32)]
        + [packed, pltpu.VMEM((WIDE * SUB, BLK), f32)]
        + [packed] * 3
        + [pltpu.VMEM((3, WIDE * SUB, BLK), f32), pltpu.VMEM((5, WIDE * SUB, BLK), f32)]
        + [pltpu.SMEM(table.shape, table.dtype) for table in tables[:-1]]
        + [pltpu.VMEM(attraction.shape, f32)]
        + [
            pltpu.SemaphoreType.DMA((strips,)),
            pltpu.SemaphoreType.DMA((strips,)),
            pltpu.SemaphoreType.DMA((4,)),
            pltpu.SemaphoreType.DMA((len(tables),)),
        ],
        compiler_params=pltpu.CompilerParams(vmem_limit_bytes=CELLS_VMEM),
        name="cells",
    )(counts, *keep_in(pltpu.HBM, *tables, moles, old_content, pressure, perm, labels, roots))
    count = lax.axis_size("dev")
    arrived = []
    for start, edge in ((0, edge_a), (1, edge_b)):
        pairs = [(i, i + 1) for i in range(start, count - 1, 2)]
        arrived.append(lax.ppermute(edge, "dev", pairs + [pair[::-1] for pair in pairs]))
    residual, step, vapour, top_aux, low_aux = pl.pallas_call(
        flux_kernel,
        out_shape=[field_shape, cell_shape, cell_shape, aux_shape, aux_shape],
        in_specs=[vmem] * len(state),
        out_specs=[hbm] * 3 + [vmem] * 2,
        scratch_shapes=[field_out, cell_pad, cell, cell]
        + [pltpu.VMEM((4, strips, layers, BLK), f32), flat, flat]
        + [pltpu.SemaphoreType.DMA(())] * 2
        + [pltpu.SemaphoreType.DMA((strips,))],
        compiler_params=pltpu.CompilerParams(vmem_limit_bytes=FLUX_VMEM),
        name="flux",
    )(*keep_in(pltpu.VMEM, *state))
    residual, step = pl.pallas_call(
        edge_kernel,
        out_shape=[field_shape, cell_shape],
        in_specs=[vmem] * 6 + [hbm] * 2,
        out_specs=[hbm] * 2,
        input_output_aliases={6: 0, 7: 1},
        scratch_shapes=[
            pltpu.VMEM((2, comps, face), f32),
            pltpu.VMEM((2, SUB, face), f32),
            pltpu.SemaphoreType.DMA((4,)),
        ],
        compiler_params=pltpu.CompilerParams(vmem_limit_bytes=16 * 1024 * 1024),
        name="edges",
    )(edge_a, edge_b, top_aux, low_aux, *arrived, residual, step)
    return (residual, step, vapour)


def solution(mesh):
    in_specs = (
        P(None, "dev", None),
        P(None, "dev", None),
        P("dev", None),
        P("dev", None),
        P("dev", None),
        P("dev", None),
        P("dev"),
        P("dev"),
        P(),
        P(),
        P(),
    )
    out_specs = (P(None, "dev", None), P("dev", None), P("dev", None))
    return jax.shard_map(
        on_device, mesh=mesh, in_specs=in_specs, out_specs=out_specs, check_vma=False
    )
```

profile of v0, /device:TPU:1, one launch (start us, length us, event | category | flops | bytes accessed | tf_op | source)
XLA Modules:
  0.0 27.8 jit_solution(14310919530743891396)
XLA Ops:
  1.3 15.6 %cells.1 = (f32[32,1024]{1,0:T(8,128)S(1)}, f32[32,1024]{1,0:T(8,128)S(1)}, f32[18,520,128]{2,1,0:T(8,128)S(1)}, f32[18,520,128]{2,1,0:T(8,128)S(1)}, f32[18,808...) custom-call(s32[1]{0:T(128)S(6)} %copy.18.counts, ...), custom_call_target="tpu_custom_call" | custom-call | tf_op jit(solution)/shard_map/cells/pallas_call | solution.py:739
  16.9 0.1 collective-permute-start
  17.0 4.3 %collective-permute-start.1 = (f32[32,1024]{1,0:T(8,128)S(1)}, f32[32,1024]{1,0:T(8,128)S(1)}, u32[]{:S(2)}, u32[]{:S(2)}) collective-permute-start(f32[32,1024]{1,0:T(8,128)S(1)} %get-tuple-element.22.edge_b), channel_id=1, source_target_pairs={{1,2},{3,4},{5,6},{7,8},{9,10},{11,12},{13,14},{15,16},{17,18},{19... | collective-permute-start | bytes 393224 | tf_op jit(solution)/shard_map/ppermute | solution.py:766
  21.3 5.4 %flux.1 = (f32[18,64,1024]{2,1,0:T(8,128)}, f32[64,1024]{1,0:T(8,128)}, f32[64,1024]{1,0:T(8,128)}, f32[26,1024]{1,0:T(8,128)S(1)}, f32[26,1024]{1,0:T(8,128)S(1)}) custom-call(f32[18,520,128]{2,1,0:T(8,128)S(1)} %get-tuple-element.23.held, f32[18,520,128]{2,1,0:T(8,128)S(1)} %get-tuple-element.24.old, f32[18,808,128]{2,1,0:T(8,128)S(1)} %get-tuple-element.25.mobile, ...), custom_call_target="tpu_custom_call" | custom-call | tf_op jit(solution)/shard_map/flux/pallas_call | solution.py:767
  26.7 0.0 collective-permute-done.in_even
  26.7 0.0 collective-permute-done.1.in_odd
  26.7 1.0 %edges.1 = (f32[18,64,1024]{2,1,0:T(8,128)}, f32[64,1024]{1,0:T(8,128)}) custom-call(f32[32,1024]{1,0:T(8,128)S(1)} %get-tuple-element.21.edge_a, f32[32,1024]{1,0:T(8,128)S(1)} %get-tuple-element.22.edge_b, f32[26,1024]{1,0:T(8,128)S(1)} %get-tuple-element.32.top_aux, ...), custom_call_target="tpu_custom_call", output_to_operand_aliasing={{0}: (6, {}), {1}: (7, {})} | custom-call | tf_op jit(solution)/shard_map/edges/pallas_call | solution.py:779
Async XLA Ops:
  16.9 9.8 %collective-permute-start = (f32[32,1024]{1,0:T(8,128)S(1)}, f32[32,1024]{1,0:T(8,128)S(1)}, u32[]{:S(2)}, u32[]{:S(2)}) collective-permute-start(f32[32,1024]{1,0:T(8,128)S(1)} %get-tuple-element.21.edge_a), channel_id=1, source_target_pairs={{0,1},{2,3},{4,5},{6,7},{8,9},{10,11},{12,13},{14,15},{16,17},{18,... | collective-permute-start | bytes 393224 | tf_op jit(solution)/shard_map/ppermute | solution.py:766
  17.0 9.7 %collective-permute-start.1 = (f32[32,1024]{1,0:T(8,128)S(1)}, f32[32,1024]{1,0:T(8,128)S(1)}, u32[]{:S(2)}, u32[]{:S(2)}) collective-permute-start(f32[32,1024]{1,0:T(8,128)S(1)} %get-tuple-element.22.edge_b), channel_id=1, source_target_pairs={{1,2},{3,4},{5,6},{7,8},{9,10},{11,12},{13,14},{15,16},{17,18},{19... | collective-permute-start | bytes 393224 | tf_op jit(solution)/shard_map/ppermute | solution.py:766
where the time goes:
time: 27.9 us; the launch traced here: 27.8 us
  Pallas kernels  22 us (79%)
  starting transfers between devices  4.4 us (16%)
  between operations  1.33 us (5%)
    pallas_call x1, Pallas kernels, on_device(): pl.pallas_call(cells_kernel, out_shape=[edge_shape, edge_shape] + held_ty...  15.6 us
    pallas_call x1, Pallas kernels, on_device(): pl.pallas_call(flux_kernel, out_shape=[field_shape, cell_shape, cell_shap...  5.39 us
    ppermute x2, starting transfers between devices, on_device(): lax.ppermute(edge, 'dev', pairs + [pair[::-1] for pair in pairs])  4.4 us
    pallas_call x1, Pallas kernels, on_device(): pl.pallas_call(edge_kernel, out_shape=[field_shape, cell_shape], in_specs...  1.03 us
  transfers between devices with their start and end apart: 2, of which 0 were waited for; matrix products, arithmetic and copies ran while one was open for 0% of the time, Pallas kernels for 19%

commit v1 on v0

--- a/solution.py
+++ b/solution.py
@@ -50,26 +50,38 @@
 
 
 def widen(wide, attraction, covolume, comps):
-    cols = comps * SUB
-    group = lax.broadcasted_iota(jnp.int32, (comps, cols), 1) // SUB
-    spread = jnp.where(group == lax.broadcasted_iota(jnp.int32, (comps, cols), 0), 1.0, 0.0)
+    cols = 3 * comps * SUB
+    span = 2 * SUB
+
+    def column(rows):
+        at = lax.broadcasted_iota(jnp.int32, (rows, cols), 1)
+        pair = at // (3 * span)
+        within = at - pair * (3 * span)
+        part = within // span
+        within = within - part * span
+        return 2 * pair + within // SUB, part, lax.rem(within, SUB)
+
+    comp, _, _ = column(comps)
+    spread = jnp.where(comp == lax.broadcasted_iota(jnp.int32, (comps, cols), 0), 1.0, 0.0)
     table = attraction[...]
     coefficients = 0.5 * (
         lax.dot_general(table, spread, (((1,), (0,)), ((), ())), precision=lax.Precision.HIGHEST)
         + lax.dot_general(table, spread, (((0,), (0,)), ((), ())), precision=lax.Precision.HIGHEST)
     )
-    lane = lax.broadcasted_iota(jnp.int32, (SUB, cols), 1)
-    row = lax.broadcasted_iota(jnp.int32, (SUB, cols), 0)
-    diagonal = lane - (lane // SUB) * SUB == row
+    comp, part, sub = column(SUB)
+    diagonal = sub == lax.broadcasted_iota(jnp.int32, (SUB, cols), 0)
     zero = jnp.zeros((SUB, cols), jnp.float32)
     of_cov = zero
     for j in range(comps):
-        of_cov = jnp.where(lane // SUB == j, covolume[j], of_cov)
+        of_cov = jnp.where(comp == j, covolume[j], of_cov)
     blocks = [coefficients[i : i + 1, :] for i in range(comps)] + [of_cov, zero + 1.0]
     for pair in range(len(blocks) // 2):
-        rows = [jnp.where(diagonal, blocks[i], zero) for i in (2 * pair, 2 * pair + 1)]
-        high, low = split_halves(jnp.concatenate(rows, 0))
-        wide[2 * SUB * pair : 2 * SUB * (pair + 1), :] = jnp.concatenate([high, low, high], 1)
+        rows = []
+        for i in (2 * pair, 2 * pair + 1):
+            value = jnp.where(diagonal, blocks[i], zero)
+            high = value.astype(jnp.bfloat16).astype(jnp.float32)
+            rows.append(jnp.where(part == 1, value - high, high))
+        wide[span * pair : span * (pair + 1), :] = jnp.concatenate(rows, 0).astype(jnp.bfloat16)
 
 
 def rows_of(g):
@@ -148,6 +160,7 @@
     vapour,
     out_cell,
     found,
+    mix,
     block_ids,
     wilson,
     covolume,
@@ -221,20 +234,21 @@
 
     cols = comps * SUB
 
-    def mixture(tile, count, keep=None):
+    def mixture(tile, count, keep=None, between=None):
         parts = ([], [], [])
         for g in range(0, count, 2):
-            highs, lows = [], []
+            if between is not None:
+                between()
+            halves = []
             for j in range(comps // 2):
                 both = [
                     jnp.concatenate([tile(2 * j, at), tile(2 * j + 1, at)], 0) for at in (g, g + 1)
                 ]
                 high, low = split_halves(jnp.concatenate(both, 1))
-                highs.append(high)
-                lows.append(low)
+                halves += [high, high, low]
             result = jnp.dot(
                 w_wide[...],
-                jnp.concatenate(highs + highs + lows, 0),
+                jnp.concatenate(halves, 0),
                 preferred_element_type=jnp.float32,
             )
             if keep is not None:
@@ -264,30 +278,57 @@
     def padded_of(k):
         return pl.ds(pl.multiple_of((k + 1) * padded + SUB, SUB), layers)
 
-    def single(k, carry):
+    def products(k, between=None):
         strip_in(moles_hbm, held, in_sem, k).wait()
         strip_in(old_hbm, old, old_sem, k).start()
-        amount, b_sum, quad = mixture(
-            lambda i, g: held[i, pl.ds(pl.multiple_of(k * layers + g * SUB, SUB), SUB), :], groups
+        return mixture(
+            lambda i, g: held[i, pl.ds(pl.multiple_of(k * layers + g * SUB, SUB), SUB), :],
+            groups,
+            between=between,
         )
-        pressure = pres[k + 1, inside, :]
-        inv_amount = recip(amount)
-        big_a = pressure * quad * inv_amount * inv_amount
-        big_b = pressure * b_sum * inv_amount
-        is_vapour = roots[:, lanes_of(k)] == 1
-        (z_factor,) = roots_of((big_a, big_b, is_vapour))
-        rho = pressure * recip(z_factor)
+
+    class Roots:
+        def __init__(self, k, amount, b_sum, quad):
+            self.pressure = pres[k + 1, inside, :]
+            self.amount = amount
+            inv_amount = recip(amount)
+            big_a = self.pressure * quad * inv_amount * inv_amount
+            self.big_b = self.pressure * b_sum * inv_amount
+            self.found, self.step = cubic(big_a, self.big_b, roots[:, lanes_of(k)] == 1)
+            self.steps = 0
+
+        def advance(self):
+            if self.steps < Z_ITERS:
+                self.found = self.step(self.found)
+                self.steps += 1
+
+    def fields(k, it):
+        while it.steps < Z_ITERS:
+            it.advance()
+        rho = it.pressure * recip(it.found - it.big_b)
         part = labels[:, lanes_of(k)].astype(jnp.float32)
         move = ((1.0 - part) * (1.0 - part) + 4.0 * part * part) * rho
         vap[k] = part
         scale[k] = rho
-        csum[k] = amount * rho
-        lam[k + 1, inside, :] = amount * move
+        csum[k] = it.amount * rho
+        lam[k + 1, inside, :] = it.amount * move
         for i in range(comps):
             mobile[i, padded_of(k), :] = held[i, strip_of(k), :] * move
+
+    def keep_mix(values):
+        for n, value in enumerate(values):
+            mix[n] = value
+
+    def single(k, carry):
+        it = Roots(k - 1, *(mix[n] for n in range(3)))
+        now = products(k, it.advance)
+        fields(k - 1, it)
+        keep_mix(now)
         return carry
 
-    lax.fori_loop(0, strips, single, 0)
+    keep_mix(products(0))
+    lax.fori_loop(1, strips, single, 0)
+    fields(strips - 1, Roots(strips - 1, *(mix[n] for n in range(3))))
 
     batch = WIDE * SUB
     own_count = counts[0]
@@ -748,6 +789,7 @@
         + [packed, pltpu.VMEM((WIDE * SUB, BLK), f32)]
         + [packed] * 3
         + [pltpu.VMEM((3, WIDE * SUB, BLK), f32), pltpu.VMEM((5, WIDE * SUB, BLK), f32)]
+        + [pltpu.VMEM((3, layers, BLK), f32)]
         + [pltpu.SMEM(table.shape, table.dtype) for table in tables[:-1]]
         + [pltpu.VMEM(attraction.shape, f32)]
         + [

time: 27.9 us -> 27.4 us (0.982)
  the two profiles are of different devices: /device:TPU:1 before, /device:TPU:16 now
where the time goes in v1:
time: 27.4 us; the launch traced here: 27.6 us
  Pallas kernels  21.9 us (80%)
  starting transfers between devices  4.35 us (16%)
  between operations  1.33 us (5%)
    pallas_call x1, Pallas kernels, on_device(): pl.pallas_call(cells_kernel, out_shape=[edge_shape, edge_shape] + held_ty...  15.5 us
    pallas_call x1, Pallas kernels, on_device(): pl.pallas_call(flux_kernel, out_shape=[field_shape, cell_shape, cell_shap...  5.39 us
    ppermute x2, starting transfers between devices, on_device(): lax.ppermute(edge, 'dev', pairs + [pair[::-1] for pair in pairs])  4.35 us
    pallas_call x1, Pallas kernels, on_device(): pl.pallas_call(edge_kernel, out_shape=[field_shape, cell_shape], in_specs...  1.03 us
  transfers between devices with their start and end apart: 2, of which 0 were waited for; matrix products, arithmetic and copies ran while one was open for 0% of the time, Pallas kernels for 20%

profile of v1, /device:TPU:16, one launch (start us, length us, event | category | flops | bytes accessed | tf_op | source)
XLA Modules:
  0.0 27.6 jit_solution(9966973245247985806)
XLA Ops:
  1.3 15.5 %cells.1 = (f32[32,1024]{1,0:T(8,128)S(1)}, f32[32,1024]{1,0:T(8,128)S(1)}, f32[18,520,128]{2,1,0:T(8,128)S(1)}, f32[18,520,128]{2,1,0:T(8,128)S(1)}, f32[18,808...) custom-call(s32[1]{0:T(128)S(6)} %copy.18.counts, ...), custom_call_target="tpu_custom_call" | custom-call | tf_op jit(solution)/shard_map/cells/pallas_call | solution.py:780
  16.7 0.1 collective-permute-start
  16.8 4.3 %collective-permute-start.1 = (f32[32,1024]{1,0:T(8,128)S(1)}, f32[32,1024]{1,0:T(8,128)S(1)}, u32[]{:S(2)}, u32[]{:S(2)}) collective-permute-start(f32[32,1024]{1,0:T(8,128)S(1)} %get-tuple-element.22.edge_b), channel_id=1, source_target_pairs={{1,2},{3,4},{5,6},{7,8},{9,10},{11,12},{13,14},{15,16},{17,18},{19... | collective-permute-start | bytes 393224 | tf_op jit(solution)/shard_map/ppermute | solution.py:808
  21.1 5.4 %flux.1 = (f32[18,64,1024]{2,1,0:T(8,128)}, f32[64,1024]{1,0:T(8,128)}, f32[64,1024]{1,0:T(8,128)}, f32[26,1024]{1,0:T(8,128)S(1)}, f32[26,1024]{1,0:T(8,128)S(1)}) custom-call(f32[18,520,128]{2,1,0:T(8,128)S(1)} %get-tuple-element.23.held, f32[18,520,128]{2,1,0:T(8,128)S(1)} %get-tuple-element.24.old, f32[18,808,128]{2,1,0:T(8,128)S(1)} %get-tuple-element.25.mobile, ...), custom_call_target="tpu_custom_call" | custom-call | tf_op jit(solution)/shard_map/flux/pallas_call | solution.py:809
  26.5 0.0 collective-permute-done.in_even
  26.5 0.0 collective-permute-done.1.in_odd
  26.5 1.0 %edges.1 = (f32[18,64,1024]{2,1,0:T(8,128)}, f32[64,1024]{1,0:T(8,128)}) custom-call(f32[32,1024]{1,0:T(8,128)S(1)} %get-tuple-element.21.edge_a, f32[32,1024]{1,0:T(8,128)S(1)} %get-tuple-element.22.edge_b, f32[26,1024]{1,0:T(8,128)S(1)} %get-tuple-element.32.top_aux, ...), custom_call_target="tpu_custom_call", output_to_operand_aliasing={{0}: (6, {}), {1}: (7, {})} | custom-call | tf_op jit(solution)/shard_map/edges/pallas_call | solution.py:821
Async XLA Ops:
  16.7 9.8 %collective-permute-start = (f32[32,1024]{1,0:T(8,128)S(1)}, f32[32,1024]{1,0:T(8,128)S(1)}, u32[]{:S(2)}, u32[]{:S(2)}) collective-permute-start(f32[32,1024]{1,0:T(8,128)S(1)} %get-tuple-element.21.edge_a), channel_id=1, source_target_pairs={{0,1},{2,3},{4,5},{6,7},{8,9},{10,11},{12,13},{14,15},{16,17},{18,... | collective-permute-start | bytes 393224 | tf_op jit(solution)/shard_map/ppermute | solution.py:808
  16.8 9.7 %collective-permute-start.1 = (f32[32,1024]{1,0:T(8,128)S(1)}, f32[32,1024]{1,0:T(8,128)S(1)}, u32[]{:S(2)}, u32[]{:S(2)}) collective-permute-start(f32[32,1024]{1,0:T(8,128)S(1)} %get-tuple-element.22.edge_b), channel_id=1, source_target_pairs={{1,2},{3,4},{5,6},{7,8},{9,10},{11,12},{13,14},{15,16},{17,18},{19... | collective-permute-start | bytes 393224 | tf_op jit(solution)/shard_map/ppermute | solution.py:808

commit v2 on v1

--- a/solution.py
+++ b/solution.py
@@ -13,6 +13,7 @@
 RR_ITERS = 3
 Z_ITERS = 5
 WIDE = 8
+AHEAD = 3
 LOG2E = math.log2(math.e)
 CELLS_VMEM = 32 * 1024 * 1024
 FLUX_VMEM = 32 * 1024 * 1024
@@ -204,10 +205,12 @@
             )
         )
     ]
-    for copy in table_copies + cell_copies:
+    for copy in table_copies:
         copy.start()
-    for k in range(strips):
+    for k in range(min(AHEAD, strips)):
         strip_in(moles_hbm, held, in_sem, k).start()
+    for copy in cell_copies:
+        copy.start()
 
     zero_tile = jnp.zeros((SUB, BLK), jnp.float32)
     zero_strip = jnp.zeros((padded, BLK), jnp.float32)
@@ -269,18 +272,17 @@
             [sums[rows, g * BLK : (g + 1) * BLK] for g in range(start, start + count)], 0
         )
 
-    for copy in cell_copies:
-        copy.wait()
-    for k in range(strips):
-        pres[k + 1, inside, :] = pres_flat[:, k * BLK : (k + 1) * BLK]
-        perm[k + 1, inside, :] = perm_flat[:, k * BLK : (k + 1) * BLK]
 
     def padded_of(k):
         return pl.ds(pl.multiple_of((k + 1) * padded + SUB, SUB), layers)
 
     def products(k, between=None):
         strip_in(moles_hbm, held, in_sem, k).wait()
-        strip_in(old_hbm, old, old_sem, k).start()
+
+        @pl.when(k + AHEAD < strips)
+        def _():
+            strip_in(moles_hbm, held, in_sem, k + AHEAD).start()
+
         return mixture(
             lambda i, g: held[i, pl.ds(pl.multiple_of(k * layers + g * SUB, SUB), SUB), :],
             groups,
@@ -327,7 +329,14 @@
         return carry
 
     keep_mix(products(0))
+    for copy in cell_copies:
+        copy.wait()
+    for k in range(strips):
+        pres[k + 1, inside, :] = pres_flat[:, k * BLK : (k + 1) * BLK]
+        perm[k + 1, inside, :] = perm_flat[:, k * BLK : (k + 1) * BLK]
     lax.fori_loop(1, strips, single, 0)
+    for k in range(strips):
+        strip_in(old_hbm, old, old_sem, k).start()
     fields(strips - 1, Roots(strips - 1, *(mix[n] for n in range(3))))
 
     batch = WIDE * SUB

time: 27.4 us -> 27.4 us (level)
  the two profiles are of different devices: /device:TPU:16 before, /device:TPU:24 now
where the time goes in v2:
time: 27.4 us; the launch traced here: 27.1 us
  Pallas kernels  16.4 us (60%)
  starting transfers between devices  9.4 us (34%)
  between operations  1.32 us (5%)
    pallas_call x1, Pallas kernels, on_device(): pl.pallas_call(cells_kernel, out_shape=[edge_shape, edge_shape] + held_ty...  9.98 us
    ppermute x2, starting transfers between devices, on_device(): lax.ppermute(edge, 'dev', pairs + [pair[::-1] for pair in pairs])  9.4 us
    pallas_call x1, Pallas kernels, on_device(): pl.pallas_call(flux_kernel, out_shape=[field_shape, cell_shape, cell_shap...  5.39 us
    pallas_call x1, Pallas kernels, on_device(): pl.pallas_call(edge_kernel, out_shape=[field_shape, cell_shape], in_specs...  1.03 us
  transfers between devices with their start and end apart: 2, of which 0 were waited for; matrix products, arithmetic and copies ran while one was open for 0% of the time, Pallas kernels for 20%

profile of v2, /device:TPU:24, one launch (start us, length us, event | category | flops | bytes accessed | tf_op | source)
XLA Modules:
  0.0 27.1 jit_solution(1999612993524446407)
XLA Ops:
  1.3 10.0 %cells.1 = (f32[32,1024]{1,0:T(8,128)S(1)}, f32[32,1024]{1,0:T(8,128)S(1)}, f32[18,520,128]{2,1,0:T(8,128)S(1)}, f32[18,520,128]{2,1,0:T(8,128)S(1)}, f32[18,808...) custom-call(s32[1]{0:T(128)S(6)} %copy.18.counts, ...), custom_call_target="tpu_custom_call" | custom-call | tf_op jit(solution)/shard_map/cells/pallas_call | solution.py:789
  11.3 4.8 %collective-permute-start = (f32[32,1024]{1,0:T(8,128)S(1)}, f32[32,1024]{1,0:T(8,128)S(1)}, u32[]{:S(2)}, u32[]{:S(2)}) collective-permute-start(f32[32,1024]{1,0:T(8,128)S(1)} %get-tuple-element.21.edge_a), channel_id=1, source_target_pairs={{0,1},{2,3},{4,5},{6,7},{8,9},{10,11},{12,13},{14,15},{16,17},{18,... | collective-permute-start | bytes 393224 | tf_op jit(solution)/shard_map/ppermute | solution.py:817
  16.1 4.6 %collective-permute-start.1 = (f32[32,1024]{1,0:T(8,128)S(1)}, f32[32,1024]{1,0:T(8,128)S(1)}, u32[]{:S(2)}, u32[]{:S(2)}) collective-permute-start(f32[32,1024]{1,0:T(8,128)S(1)} %get-tuple-element.22.edge_b), channel_id=1, source_target_pairs={{1,2},{3,4},{5,6},{7,8},{9,10},{11,12},{13,14},{15,16},{17,18},{19... | collective-permute-start | bytes 393224 | tf_op jit(solution)/shard_map/ppermute | solution.py:817
  20.7 5.4 %flux.1 = (f32[18,64,1024]{2,1,0:T(8,128)}, f32[64,1024]{1,0:T(8,128)}, f32[64,1024]{1,0:T(8,128)}, f32[26,1024]{1,0:T(8,128)S(1)}, f32[26,1024]{1,0:T(8,128)S(1)}) custom-call(f32[18,520,128]{2,1,0:T(8,128)S(1)} %get-tuple-element.23.held, f32[18,520,128]{2,1,0:T(8,128)S(1)} %get-tuple-element.24.old, f32[18,808,128]{2,1,0:T(8,128)S(1)} %get-tuple-element.25.mobile, ...), custom_call_target="tpu_custom_call" | custom-call | tf_op jit(solution)/shard_map/flux/pallas_call | solution.py:818
  26.1 0.0 collective-permute-done.in_even
  26.1 0.0 collective-permute-done.1.in_odd
  26.1 1.0 %edges.1 = (f32[18,64,1024]{2,1,0:T(8,128)}, f32[64,1024]{1,0:T(8,128)}) custom-call(f32[32,1024]{1,0:T(8,128)S(1)} %get-tuple-element.21.edge_a, f32[32,1024]{1,0:T(8,128)S(1)} %get-tuple-element.22.edge_b, f32[26,1024]{1,0:T(8,128)S(1)} %get-tuple-element.32.top_aux, ...), custom_call_target="tpu_custom_call", output_to_operand_aliasing={{0}: (6, {}), {1}: (7, {})} | custom-call | tf_op jit(solution)/shard_map/edges/pallas_call | solution.py:830
Async XLA Ops:
  11.3 14.8 %collective-permute-start = (f32[32,1024]{1,0:T(8,128)S(1)}, f32[32,1024]{1,0:T(8,128)S(1)}, u32[]{:S(2)}, u32[]{:S(2)}) collective-permute-start(f32[32,1024]{1,0:T(8,128)S(1)} %get-tuple-element.21.edge_a), channel_id=1, source_target_pairs={{0,1},{2,3},{4,5},{6,7},{8,9},{10,11},{12,13},{14,15},{16,17},{18,... | collective-permute-start | bytes 393224 | tf_op jit(solution)/shard_map/ppermute | solution.py:817
  16.1 10.0 %collective-permute-start.1 = (f32[32,1024]{1,0:T(8,128)S(1)}, f32[32,1024]{1,0:T(8,128)S(1)}, u32[]{:S(2)}, u32[]{:S(2)}) collective-permute-start(f32[32,1024]{1,0:T(8,128)S(1)} %get-tuple-element.22.edge_b), channel_id=1, source_target_pairs={{1,2},{3,4},{5,6},{7,8},{9,10},{11,12},{13,14},{15,16},{17,18},{19... | collective-permute-start | bytes 393224 | tf_op jit(solution)/shard_map/ppermute | solution.py:817

commit v3 on v2

--- a/solution.py
+++ b/solution.py
@@ -64,10 +64,11 @@
 
     comp, _, _ = column(comps)
     spread = jnp.where(comp == lax.broadcasted_iota(jnp.int32, (comps, cols), 0), 1.0, 0.0)
+    spread = spread.astype(jnp.bfloat16)
     table = attraction[...]
-    coefficients = 0.5 * (
-        lax.dot_general(table, spread, (((1,), (0,)), ((), ())), precision=lax.Precision.HIGHEST)
-        + lax.dot_general(table, spread, (((0,), (0,)), ((), ())), precision=lax.Precision.HIGHEST)
+    of_high, of_low = (
+        jnp.dot(half, spread, preferred_element_type=jnp.float32)
+        for half in split_halves(0.5 * (table + table.T))
     )
     comp, part, sub = column(SUB)
     diagonal = sub == lax.broadcasted_iota(jnp.int32, (SUB, cols), 0)
@@ -75,13 +76,12 @@
     of_cov = zero
     for j in range(comps):
         of_cov = jnp.where(comp == j, covolume[j], of_cov)
-    blocks = [coefficients[i : i + 1, :] for i in range(comps)] + [of_cov, zero + 1.0]
+    cov_high = of_cov.astype(jnp.bfloat16).astype(jnp.float32)
+    taken = jnp.where(part[0:1, :] == 1, of_low, of_high)
+    blocks = [taken[i : i + 1, :] for i in range(comps)]
+    blocks += [jnp.where(part == 1, of_cov - cov_high, cov_high), jnp.where(part == 1, 0.0, 1.0)]
     for pair in range(len(blocks) // 2):
-        rows = []
-        for i in (2 * pair, 2 * pair + 1):
-            value = jnp.where(diagonal, blocks[i], zero)
-            high = value.astype(jnp.bfloat16).astype(jnp.float32)
-            rows.append(jnp.where(part == 1, value - high, high))
+        rows = [jnp.where(diagonal, blocks[i], zero) for i in (2 * pair, 2 * pair + 1)]
         wide[span * pair : span * (pair + 1), :] = jnp.concatenate(rows, 0).astype(jnp.bfloat16)
 
 
@@ -434,9 +434,9 @@
                     depart = a_mix * inv_b * (1.0 / (2.0 * SQRT_TWO)) * jnp.log(log_arg)
                     of_cov = (LOG2E * inv_b) * (z_factor - 1.0 + depart)
                     of_sum = (2.0 * LOG2E) * depart * whole * recip(quad)
-                    parts.append((of_cov, LOG2E * jnp.log(z_factor - big_b), of_sum))
+                    parts.append((of_cov, z_factor - big_b, of_sum))
                 cov_gap = parts[0][0] - parts[1][0]
-                log_gap = parts[0][1] - parts[1][1]
+                log_gap = LOG2E * jnp.log(parts[0][1] * recip(parts[1][1]))
                 for i in range(comps):
                     log2_k = (covolume[i] * cov_gap - log_gap) - (
                         parts[0][2] * total(i, 0, WIDE) - parts[1][2] * total(i, WIDE, WIDE)

time: 27.4 us -> 27.4 us (level)
  no operation moved by 1% of the time
where the time goes in v3:
time: 27.4 us; the launch traced here: 27 us
  Pallas kernels  16.4 us (60%)
  starting transfers between devices  9.29 us (34%)
  between operations  1.33 us (5%)
    pallas_call x1, Pallas kernels, on_device(): pl.pallas_call(cells_kernel, out_shape=[edge_shape, edge_shape] + held_ty...  10 us
    ppermute x2, starting transfers between devices, on_device(): lax.ppermute(edge, 'dev', pairs + [pair[::-1] for pair in pairs])  9.29 us
    pallas_call x1, Pallas kernels, on_device(): pl.pallas_call(flux_kernel, out_shape=[field_shape, cell_shape, cell_shap...  5.39 us
    pallas_call x1, Pallas kernels, on_device(): pl.pallas_call(edge_kernel, out_shape=[field_shape, cell_shape], in_specs...  1.03 us
  transfers between devices with their start and end apart: 2, of which 0 were waited for; matrix products, arithmetic and copies ran while one was open for 0% of the time, Pallas kernels for 20%

profile of v3, /device:TPU:24, one launch (start us, length us, event | category | flops | bytes accessed | tf_op | source)
XLA Modules:
  0.0 27.0 jit_solution(6319948049579147502)
XLA Ops:
  1.3 10.0 %cells.1 = (f32[32,1024]{1,0:T(8,128)S(1)}, f32[32,1024]{1,0:T(8,128)S(1)}, f32[18,520,128]{2,1,0:T(8,128)S(1)}, f32[18,520,128]{2,1,0:T(8,128)S(1)}, f32[18,808...) custom-call(s32[1]{0:T(128)S(6)} %copy.18.counts, ...), custom_call_target="tpu_custom_call" | custom-call | tf_op jit(solution)/shard_map/cells/pallas_call | solution.py:789
  11.3 0.1 collective-permute-start
  11.4 9.2 %collective-permute-start.1 = (f32[32,1024]{1,0:T(8,128)S(1)}, f32[32,1024]{1,0:T(8,128)S(1)}, u32[]{:S(2)}, u32[]{:S(2)}) collective-permute-start(f32[32,1024]{1,0:T(8,128)S(1)} %get-tuple-element.22.edge_b), channel_id=1, source_target_pairs={{1,2},{3,4},{5,6},{7,8},{9,10},{11,12},{13,14},{15,16},{17,18},{19... | collective-permute-start | bytes 393224 | tf_op jit(solution)/shard_map/ppermute | solution.py:817
  20.6 5.4 %flux.1 = (f32[18,64,1024]{2,1,0:T(8,128)}, f32[64,1024]{1,0:T(8,128)}, f32[64,1024]{1,0:T(8,128)}, f32[26,1024]{1,0:T(8,128)S(1)}, f32[26,1024]{1,0:T(8,128)S(1)}) custom-call(f32[18,520,128]{2,1,0:T(8,128)S(1)} %get-tuple-element.23.held, f32[18,520,128]{2,1,0:T(8,128)S(1)} %get-tuple-element.24.old, f32[18,808,128]{2,1,0:T(8,128)S(1)} %get-tuple-element.25.mobile, ...), custom_call_target="tpu_custom_call" | custom-call | tf_op jit(solution)/shard_map/flux/pallas_call | solution.py:818
  26.0 0.0 collective-permute-done.in_even
  26.0 0.0 collective-permute-done.1.in_odd
  26.0 1.0 %edges.1 = (f32[18,64,1024]{2,1,0:T(8,128)}, f32[64,1024]{1,0:T(8,128)}) custom-call(f32[32,1024]{1,0:T(8,128)S(1)} %get-tuple-element.21.edge_a, f32[32,1024]{1,0:T(8,128)S(1)} %get-tuple-element.22.edge_b, f32[26,1024]{1,0:T(8,128)S(1)} %get-tuple-element.32.top_aux, ...), custom_call_target="tpu_custom_call", output_to_operand_aliasing={{0}: (6, {}), {1}: (7, {})} | custom-call | tf_op jit(solution)/shard_map/edges/pallas_call | solution.py:830
Async XLA Ops:
  11.3 14.7 %collective-permute-start = (f32[32,1024]{1,0:T(8,128)S(1)}, f32[32,1024]{1,0:T(8,128)S(1)}, u32[]{:S(2)}, u32[]{:S(2)}) collective-permute-start(f32[32,1024]{1,0:T(8,128)S(1)} %get-tuple-element.21.edge_a), channel_id=1, source_target_pairs={{0,1},{2,3},{4,5},{6,7},{8,9},{10,11},{12,13},{14,15},{16,17},{18,... | collective-permute-start | bytes 393224 | tf_op jit(solution)/shard_map/ppermute | solution.py:817
  11.4 14.6 %collective-permute-start.1 = (f32[32,1024]{1,0:T(8,128)S(1)}, f32[32,1024]{1,0:T(8,128)S(1)}, u32[]{:S(2)}, u32[]{:S(2)}) collective-permute-start(f32[32,1024]{1,0:T(8,128)S(1)} %get-tuple-element.22.edge_b), channel_id=1, source_target_pairs={{1,2},{3,4},{5,6},{7,8},{9,10},{11,12},{13,14},{15,16},{17,18},{19... | collective-permute-start | bytes 393224 | tf_op jit(solution)/shard_map/ppermute | solution.py:817
